TPU v7x, 256 devices: a whole 4x4x8 slice. The times are simulated.
256 devices in a mesh: dp: 8 (over x, z_hi), ctx: 32 (over y, z_lo, core).
Axes of the slice: x: 4, y: 4, z: 8 (z_hi: 2, z_lo: 4; z = z_hi * 4 + z_lo), core: 2. Of those that a mesh axis runs over, the one named last changes fastest.
Arguments:
- layer_input: bfloat16 [8, 4096, 8192], P('dp', 'ctx'), may hold values from -6 to 6
- queries: bfloat16 [8, 4096, 1024], P('dp', 'ctx'), may hold values from -6 to 6
- keys: bfloat16 [8, 4096, 128], P('dp', 'ctx'), may hold values from -6 to 6
- values: bfloat16 [8, 4096, 128], P('dp', 'ctx'), may hold values from -6 to 6
- d_out: bfloat16 [8, 4096, 1024], P('dp', 'ctx'), may hold values from -6 to 6
- doc_lengths: int32 [8, 8], P('dp'), may hold values from 1 to 1024, 4096 in all within a row
- block_order: int32 [64], replicated, may hold values from 0 to 63, as said below
Outputs:
- query_grad: bfloat16 [8, 4096, 1024], P('dp', 'ctx')
- key_grad: bfloat16 [8, 4096, 128], P('dp', 'ctx')
- value_grad: bfloat16 [8, 4096, 128], P('dp', 'ctx')
- kv_weight_grad: float32 [32, 256, 256], P('ctx', 'dp')
Inputs may be any that keep to these rules, and one draw needn't show every extreme that they name: `block_order`: entries 2r and 2r+1 are the blocks stored in rows 2r*64 to 2r*64 + 2*64 - 1; they sum to 63, and every block appears once.
All inputs are finite; a program needn't handle non-finite values.
Results may differ from a plain program's by a relative error of at most 0.012.
Values may be sent and summed in bfloat16 or wider, within the bound.
A program may use at most 64 MiB of HBM per device.

v0:
```python
import math
import jax
import jax.numpy as jnp
from jax import lax
from jax.sharding import PartitionSpec as P

big_negative = -1e30


def per_device(layer_input, queries, keys, values, d_out, doc_lengths, block_order):
    local_len = queries.shape[1]
    head_dim = keys.shape[2]
    heads = queries.shape[2] // head_dim
    ctx_size = lax.axis_size("ctx")
    seq_len = local_len * ctx_size
    half = local_len // 2
    rank = lax.axis_index("ctx")
    scale = 1.0 / math.sqrt(head_dim)
    key_pos = (block_order[:, None] * half + jnp.arange(half, dtype=jnp.int32)[None, :]).reshape(
        seq_len
    )
    ends = jnp.cumsum(doc_lengths[0])
    key_doc = jnp.sum((key_pos[:, None] >= ends[None, :]).astype(jnp.int32), axis=1)
    query_pos = lax.dynamic_slice_in_dim(key_pos, rank * local_len, local_len)
    query_doc = lax.dynamic_slice_in_dim(key_doc, rank * local_len, local_len)
    local_rows = layer_input[0]
    all_keys, all_values = (
        lax.all_gather(keys[0], "ctx", axis=0, tiled=True),
        lax.all_gather(values[0], "ctx", axis=0, tiled=True),
    )
    block = 512
    nblocks = seq_len // block
    key_blocks = all_keys.reshape(nblocks, block, head_dim)
    value_blocks = all_values.reshape(nblocks, block, head_dim)
    pos_blocks = key_pos.reshape(nblocks, block)
    doc_blocks = key_doc.reshape(nblocks, block)
    q_heads = queries[0].reshape(local_len, heads, head_dim)
    d_heads = d_out[0].reshape(local_len, heads, head_dim)

    def visible(kpos, kdoc):
        return ((kpos[None, :] <= query_pos[:, None]) & (kdoc[None, :] == query_doc[:, None]))[None]

    def scores(kblock):
        return (
            jnp.einsum("thd,kd->htk", q_heads, kblock, preferred_element_type=jnp.float32) * scale
        )

    def prob_grads(vblock):
        return jnp.einsum("thd,kd->htk", d_heads, vblock, preferred_element_type=jnp.float32)

    def stats_step(carry, item):
        run_max, run_sum, run_dot = carry
        kblock, vblock, kpos, kdoc = item
        mask = visible(kpos, kdoc)
        s = scores(kblock)
        new_max = jnp.maximum(run_max, jnp.max(jnp.where(mask, s, big_negative), axis=2))
        terms = jnp.where(mask, jnp.exp(s - new_max[..., None]), 0.0)
        factor = jnp.exp(run_max - new_max)
        run_sum = run_sum * factor + jnp.sum(terms, axis=2)
        run_dot = run_dot * factor + jnp.sum(terms * prob_grads(vblock), axis=2)
        return ((new_max, run_sum, run_dot), None)

    items = (key_blocks, value_blocks, pos_blocks, doc_blocks)
    zeros_stat = jnp.zeros((heads, local_len), jnp.float32)
    start_stats = (jnp.full((heads, local_len), big_negative, jnp.float32), zeros_stat, zeros_stat)
    (run_max, run_sum, run_dot), _ = lax.scan(stats_step, start_stats, items)
    lse = run_max + jnp.log(run_sum)
    delta = run_dot / run_sum

    def grad_step(dq_acc, item):
        kblock, vblock, kpos, kdoc = item
        p = jnp.where(visible(kpos, kdoc), jnp.exp(scores(kblock) - lse[..., None]), 0.0)
        weights = p.astype(jnp.bfloat16)
        dprob = prob_grads(vblock)
        dscore = (p * (dprob - delta[..., None])).astype(jnp.bfloat16)
        dq_acc = dq_acc + jnp.einsum(
            "htk,kd->thd", dscore, kblock, preferred_element_type=jnp.float32
        )
        dk_part = (
            jnp.einsum("htk,thd->kd", dscore, q_heads, preferred_element_type=jnp.float32) * scale
        )
        dv_part = jnp.einsum("htk,thd->kd", weights, d_heads, preferred_element_type=jnp.float32)
        return (dq_acc, jnp.concatenate([dk_part, dv_part], axis=1))

    dq_acc, partials = lax.scan(
        grad_step, jnp.zeros((local_len, heads, head_dim), jnp.float32), items
    )
    owned = lax.psum_scatter(
        partials.reshape(seq_len, 2 * head_dim), "ctx", scatter_dimension=0, tiled=True
    )
    kv_grad = owned.astype(jnp.bfloat16)
    query_grad = (dq_acc * scale).astype(jnp.bfloat16).reshape(1, local_len, heads * head_dim)
    contract = (((0,), (0,)), ((), ()))
    exact = lax.Precision.HIGHEST
    cols = local_rows.astype(jnp.float32)
    term = lax.psum_scatter(
        lax.dot_general(cols, owned, contract, precision=exact, preferred_element_type=jnp.float32),
        "ctx",
        scatter_dimension=0,
        tiled=True,
    )
    weight_grad = lax.psum_scatter(term, "dp", scatter_dimension=0, tiled=True)
    weight_grad = weight_grad * (1.0 / math.sqrt(lax.axis_size("dp") * seq_len))
    key_grad = kv_grad[:, :head_dim].reshape(1, local_len, head_dim)
    value_grad = kv_grad[:, head_dim:].reshape(1, local_len, head_dim)
    return (
        query_grad,
        key_grad,
        value_grad,
        weight_grad.reshape(1, weight_grad.shape[0], 2 * head_dim),
    )


def solution(mesh):
    placed = (
        P("dp", "ctx", None),
        P("dp", "ctx", None),
        P("dp", "ctx", None),
        P("dp", "ctx", None),
        P("dp", "ctx", None),
        P("dp", None),
        P(),
    )
    return jax.shard_map(
        per_device,
        mesh=mesh,
        in_specs=placed,
        out_specs=(
            P("dp", "ctx", None),
            P("dp", "ctx", None),
            P("dp", "ctx", None),
            P("ctx", "dp", None),
        ),
        check_vma=False,
    )
```

profile of v0, /device:TPU:8, one launch (start us, length us, event | category | flops | bytes accessed | tf_op | source)
XLA Modules:
  0.0 636.3 jit_solution(2492663735038133514)
XLA Ops:
  11.0 1.8 copy.43
  15.2 56.2 %all-gather.5.cloned.1.call-done = bf16[1,4096,128]{2,1,0:T(8,128)(2,1)} async-done(((bf16[1,128,128]{2,1,0:T(8,128)(2,1)}), bf16[1,4096,128]{2,1,0:T(8,128)(2,1)}) %all-gather.5.cloned.1.call-update) | async-done | bytes 1048592 | tf_op jit(solution)/shard_map/all_gather | solution.py:28
  71.4 59.7 %all-gather.7.cloned.1.call-done = bf16[1,4096,128]{2,1,0:T(8,128)(2,1)} async-done(((bf16[1,128,128]{2,1,0:T(8,128)(2,1)}), bf16[1,4096,128]{2,1,0:T(8,128)(2,1)}) %all-gather.7.cloned.1.call-update) | async-done | bytes 1048592 | tf_op jit(solution)/shard_map/all_gather | solution.py:29
  131.1 29.4 %while.28 = (s32[]{:T(128)}, f32[8,128]{1,0:T(8,128)S(1)}, f32[8,128]{1,0:T(8,128)S(1)}, f32[8,128]{1,0:T(8,128)S(1)}, s32[8,512]{1,0:T(8,128)S(1)}, /*index=5*/...) while((s32[]{:T(128)}, f32[8,128]{1,0:T(8,128)S(1)}, ...), condition=%wide.region_6.7_spmd.clone, body=%wide.region_2.6_spmd.clone.sunk | while | flops 274930688 | bytes 7427236 | solution.py:66
  132.7 1.6 fusion.66
  136.4 1.6 fusion.66
  140.0 1.6 fusion.66
  143.7 1.6 fusion.66
  147.4 1.6 fusion.66
  151.0 1.6 fusion.66
  160.5 67.4 %while.29 = (s32[]{:T(128)}, f32[128,8,128]{0,2,1:T(8,128)}, f32[8,512,256]{2,1,0:T(8,128)}, bf16[8,512,128]{2,1,0:T(8,128)(2,1)}, s32[8,512]{1,0:T(8,128)S(1)},...) while((s32[]{:T(128)}, f32[128,8,128]{0,2,1:T(8,128)}, ...), condition=%wide.region_8.9_spmd.clone, body=%wide.region_7.8_spmd.clone.sunk | while | flops 675414016 | bytes 15750323 | solution.py:85
  160.7 1.6 fusion.79
  165.5 2.1 fusion.81
  168.9 1.6 fusion.79
  173.7 2.3 fusion.81
  177.3 1.6 fusion.79
  182.2 2.3 fusion.81
  185.8 1.6 fusion.79
  190.6 2.3 fusion.81
  194.3 1.6 fusion.79
  199.1 2.3 fusion.81
  202.7 1.6 fusion.79
  207.5 2.3 fusion.81
  211.1 1.6 fusion.79
  216.0 2.3 fusion.81
  219.6 1.6 fusion.79
  224.4 2.3 fusion.81
  227.9 131.9 %reduce-scatter.6.cloned.1.call-done = f32[128,256]{1,0:T(8,128)} async-done(((f32[4096,256]{1,0:T(8,128)}), f32[128,256]{1,0:T(8,128)}) %reduce-scatter.6.cloned.1.call-update) | async-done | bytes 131088 | tf_op jit(solution)/shard_map/reduce_scatter | solution.py:88
  359.8 6.6 %convolution_bitcast_fusion.3 = f32[8192,256]{0,1:T(8,128)} fusion(f32[128,256]{1,0:T(8,128)} %reduce-scatter.6.cloned.1.call-done, bf16[1,128,8192]{2,1,0:T(8,128)(2,1)S(1)} %copy-done), kind=kOutput, calls=%fused_computation.50 | convolution fusion | flops 3221225472 | bytes 10616832 | tf_op jit(solution)/shard_map/dot_general | solution.py:97
  366.5 159.5 %reduce-scatter.8.cloned.1.call-done = f32[256,256]{0,1:T(8,128)} async-done(((f32[8192,256]{0,1:T(8,128)}), f32[256,256]{0,1:T(8,128)}) %reduce-scatter.8.cloned.1.call-update) | async-done | bytes 262160 | tf_op jit(solution)/shard_map/reduce_scatter | solution.py:96
  526.0 1.8 copy.58
  530.3 97.8 %reduce-scatter.10.cloned.1.call-done = f32[32,256]{1,0:T(8,128)} async-done(((f32[256,256]{1,0:T(8,128)}), f32[32,256]{1,0:T(8,128)}) %reduce-scatter.10.cloned.1.call-update) | async-done | bytes 32784
  (166 shorter events, 65.9 us)
Async XLA Ops:
  7.2 352.6 %copy-start = (bf16[1,128,8192]{2,1,0:T(8,128)(2,1)S(1)}, bf16[1,128,8192]{2,1,0:T(8,128)(2,1)}, u32[]{:S(2)}) copy-start(bf16[1,128,8192]{2,1,0:T(8,128)(2,1)} %param.11) | copy-start | bytes 6291460
  7.2 64.2 %all-gather.5.cloned.1.call-start = ((), (), s32[]{:S(2)}) async-start(), calls=%async_computation.5 | async-start | bytes 1081344 | tf_op jit(solution)/shard_map/all_gather | solution.py:28
  7.9 123.2 %all-gather.7.cloned.1.call-start = ((), (), s32[]{:S(2)}) async-start(), calls=%async_computation.6 | async-start | bytes 1081344 | tf_op jit(solution)/shard_map/all_gather | solution.py:29
  8.7 351.1 %reduce-scatter.6.cloned.1.call-start = ((), (), s32[]{:S(2)}) async-start(), calls=%async_computation.3 | async-start | bytes 4325376 | tf_op jit(solution)/shard_map/reduce_scatter | solution.py:88
  227.8 298.1 %reduce-scatter.8.cloned.1.call-start = ((), (), s32[]{:S(2)}) async-start(), calls=%async_computation.4 | async-start | bytes 8650752 | tf_op jit(solution)/shard_map/reduce_scatter | solution.py:96
  366.4 163.3 %copy-start.1 = (f32[128,256]{1,0:T(8,128)S(1)}, f32[128,256]{1,0:T(8,128)}, u32[]{:S(2)}) copy-start(f32[128,256]{1,0:T(8,128)} %reduce-scatter.6.cloned.1.call-done) | copy-start | bytes 393220
  366.4 261.8 %reduce-scatter.10.cloned.1.call-start = ((), (), s32[]{:S(2)}) async-start(), calls=%async_computation.7 | async-start | bytes 294912
Sparse Core Ops, SparseCore 0:
  9.9 61.4 all-gather.4
  73.3 57.7 all-gather.6
  228.0 131.8 reduce-scatter.5
  366.5 159.3 reduce-scatter.7
  529.6 98.4 reduce-scatter.9
where the time goes:
time: 638 us; the launch traced here: 636 us
  waiting for transfers between devices  506 us (79%)
  matrix products  86.7 us (14%)
  local copies, waits for them, and re-layouts  18 us (3%)
  between operations  13.9 us (2%)
  other arithmetic  9.99 us (2%)
    reduce_scatter x1, waiting for transfers between devices, per_device(): lax.psum_scatter(lax.dot_general(cols, owned, contract, precision=exact,...  159 us
    reduce_scatter x1, waiting for transfers between devices, per_device(): lax.psum_scatter(partials.reshape(seq_len, 2 * head_dim), 'ctx', scatter_...  132 us
    unnamed x6, waiting for transfers between devices  99.2 us
    all_gather x1, waiting for transfers between devices, per_device(): lax.all_gather(values[0], 'ctx', axis=0, tiled=True)  59.7 us
    all_gather x1, waiting for transfers between devices, per_device(): lax.all_gather(keys[0], 'ctx', axis=0, tiled=True)  56.2 us
    dot_general x16, matrix products, scores(): jnp.einsum('thd,kd->htk', q_heads, kblock, preferred_element_type=jnp.flo...  23.5 us
    dot_general x16, matrix products, prob_grads(): jnp.einsum('thd,kd->htk', d_heads, vblock, preferred_element_type=jnp.flo...  23.1 us
    dot_general x8, matrix products, grad_step(): jnp.einsum('htk,kd->thd', dscore, kblock, preferred_element_type=jnp.floa...  18.3 us
  transfers between devices with their start and end apart: 5, of which 5 were waited for; matrix products, arithmetic and copies ran while one was open for 1% of the time, Pallas kernels for 0%

commit v1 on v0

--- a/solution.py
+++ b/solution.py
@@ -24,9 +24,12 @@
     query_pos = lax.dynamic_slice_in_dim(key_pos, rank * local_len, local_len)
     query_doc = lax.dynamic_slice_in_dim(key_doc, rank * local_len, local_len)
     local_rows = layer_input[0]
+    save_plane = lambda xin: jnp.concatenate(
+        jax.lax.all_to_all(jnp.stack(jax.lax.axis_size("ctx") * [xin], axis=0), "ctx", 0, 0), axis=0
+    )
     all_keys, all_values = (
         lax.all_gather(keys[0], "ctx", axis=0, tiled=True),
-        lax.all_gather(values[0], "ctx", axis=0, tiled=True),
+        save_plane(values[0]),
     )
     block = 512
     nblocks = seq_len // block

time: 638 us -> 581 us (0.911)
  waiting for transfers between devices: 506 us -> 442 us
  starting transfers between devices: 0.2 us -> 9.36 us
    all_gather x1 -> x0, waiting for transfers between devices: 59.7 us -> none  [per_device(): lax.all_gather(values[0], 'ctx', axis=0, tiled=True)]
    all_to_all x0 -> x1, starting transfers between devices: none -> 9.19 us  [per_device(): jax.lax.all_to_all(jnp.stack(jax.lax.axis_size('ctx') * [xin], axis=0), '...]
    unnamed x6 -> x5, waiting for transfers between devices: 99.2 us -> 98.6 us
  transfers between devices with their start and end apart: 5 -> 5, of which waited for: 5 -> 4; matrix products, arithmetic and copies ran while one was open for 1% -> 1% of each run, Pallas kernels for 0% -> 0%
where the time goes in v1:
time: 581 us; the launch traced here: 580 us
  waiting for transfers between devices  442 us (76%)
  matrix products  86.6 us (15%)
  local copies, waits for them, and re-layouts  18.1 us (3%)
  between operations  13.9 us (2%)
  starting transfers between devices  9.36 us (2%)
  other arithmetic  8.69 us (1%)
    reduce_scatter x1, waiting for transfers between devices, per_device(): lax.psum_scatter(lax.dot_general(cols, owned, contract, precision=exact,...  159 us
    reduce_scatter x1, waiting for transfers between devices, per_device(): lax.psum_scatter(partials.reshape(seq_len, 2 * head_dim), 'ctx', scatter_...  132 us
    unnamed x5, waiting for transfers between devices  98.6 us
    all_gather x1, waiting for transfers between devices, per_device(): lax.all_gather(keys[0], 'ctx', axis=0, tiled=True)  52.6 us
    dot_general x16, matrix products, scores(): jnp.einsum('thd,kd->htk', q_heads, kblock, preferred_element_type=jnp.flo...  23.5 us
    dot_general x16, matrix products, prob_grads(): jnp.einsum('thd,kd->htk', d_heads, vblock, preferred_element_type=jnp.flo...  23.1 us
    dot_general x8, matrix products, grad_step(): jnp.einsum('htk,kd->thd', dscore, kblock, preferred_element_type=jnp.floa...  18.2 us
  transfers between devices with their start and end apart: 5, of which 4 were waited for; matrix products, arithmetic and copies ran while one was open for 1% of the time, Pallas kernels for 0%

profile of v1, /device:TPU:8, one launch (start us, length us, event | category | flops | bytes accessed | tf_op | source)
XLA Modules:
  0.0 579.9 jit_solution(1777726183831004694)
XLA Ops:
  8.0 2.0 stack.3
  10.0 9.2 %all-to-all-start = ((bf16[32,128,128]{2,1,0:T(8,128)(2,1)}), bf16[32,128,128]{2,1,0:T(8,128)(2,1)}, u32[]{:S(2)}, u32[]{:S(2)}) async-start(bf16[32,128,128]{2,1,0:T(8,128)(2,1)} %stack.3), calls=%async_computation | async-start | bytes 2097152 | tf_op jit(solution)/shard_map/all_to_all | solution.py:28
  22.6 52.6 %all-gather.3.cloned.1.call-done = bf16[1,4096,128]{2,1,0:T(8,128)(2,1)} async-done(((bf16[1,128,128]{2,1,0:T(8,128)(2,1)}), bf16[1,4096,128]{2,1,0:T(8,128)(2,1)}) %all-gather.3.cloned.1.call-update) | async-done | bytes 1048592 | tf_op jit(solution)/shard_map/all_gather | solution.py:31
  75.2 29.4 %while.28 = (s32[]{:T(128)}, f32[8,128]{1,0:T(8,128)S(1)}, f32[8,128]{1,0:T(8,128)S(1)}, f32[8,128]{1,0:T(8,128)S(1)}, s32[8,512]{1,0:T(8,128)S(1)}, /*index=5*/...) while((s32[]{:T(128)}, f32[8,128]{1,0:T(8,128)S(1)}, ...), condition=%wide.region_6.7_spmd.clone, body=%wide.region_2.6_spmd.clone.sunk | while | flops 274930688 | bytes 7427236 | solution.py:69
  76.8 1.6 fusion.66
  80.5 1.6 fusion.66
  84.2 1.6 fusion.66
  87.8 1.6 fusion.66
  91.5 1.6 fusion.66
  95.2 1.6 fusion.66
  104.6 67.3 %while.29 = (s32[]{:T(128)}, f32[128,8,128]{0,2,1:T(8,128)}, f32[8,512,256]{2,1,0:T(8,128)}, bf16[8,512,128]{2,1,0:T(8,128)(2,1)}, s32[8,512]{1,0:T(8,128)S(1)},...) while((s32[]{:T(128)}, f32[128,8,128]{0,2,1:T(8,128)}, ...), condition=%wide.region_8.9_spmd.clone, body=%wide.region_7.8_spmd.clone.sunk | while | flops 675414016 | bytes 15750323 | solution.py:88
  104.8 1.6 fusion.79
  109.7 2.1 fusion.81
  113.1 1.6 fusion.79
  117.9 2.3 fusion.81
  121.5 1.6 fusion.79
  126.3 2.3 fusion.81
  129.9 1.6 fusion.79
  134.8 2.3 fusion.81
  138.4 1.6 fusion.79
  143.2 2.3 fusion.81
  146.8 1.6 fusion.79
  151.6 2.3 fusion.81
  155.3 1.6 fusion.79
  160.1 2.3 fusion.81
  163.7 1.6 fusion.79
  168.5 2.3 fusion.81
  172.0 132.1 %reduce-scatter.6.cloned.1.call-done = f32[128,256]{1,0:T(8,128)} async-done(((f32[4096,256]{1,0:T(8,128)}), f32[128,256]{1,0:T(8,128)}) %reduce-scatter.6.cloned.1.call-update) | async-done | bytes 131088 | tf_op jit(solution)/shard_map/reduce_scatter | solution.py:91
  304.1 6.5 %convolution_bitcast_fusion.3 = f32[8192,256]{0,1:T(8,128)} fusion(f32[128,256]{1,0:T(8,128)} %reduce-scatter.6.cloned.1.call-done, bf16[1,128,8192]{2,1,0:T(8,128)(2,1)S(1)} %copy-done), kind=kOutput, calls=%fused_computation.50 | convolution fusion | flops 3221225472 | bytes 10616832 | tf_op jit(solution)/shard_map/dot_general | solution.py:100
  310.7 158.8 %reduce-scatter.8.cloned.1.call-done = f32[256,256]{0,1:T(8,128)} async-done(((f32[8192,256]{0,1:T(8,128)}), f32[256,256]{0,1:T(8,128)}) %reduce-scatter.8.cloned.1.call-update) | async-done | bytes 262160 | tf_op jit(solution)/shard_map/reduce_scatter | solution.py:99
  469.5 1.8 copy.58
  473.9 97.9 %reduce-scatter.10.cloned.1.call-done = f32[32,256]{1,0:T(8,128)} async-done(((f32[256,256]{1,0:T(8,128)}), f32[32,256]{1,0:T(8,128)}) %reduce-scatter.10.cloned.1.call-update) | async-done | bytes 32784
  (174 shorter events, 63.8 us)
Async XLA Ops:
  7.2 296.9 %copy-start = (bf16[1,128,8192]{2,1,0:T(8,128)(2,1)S(1)}, bf16[1,128,8192]{2,1,0:T(8,128)(2,1)}, u32[]{:S(2)}) copy-start(bf16[1,128,8192]{2,1,0:T(8,128)(2,1)} %param.11) | copy-start | bytes 6291460
  7.2 12.1 %copy-start.4 = (s32[1,8]{1,0:T(1,128)S(1)}, s32[1,8]{1,0:T(1,128)}, u32[]{:S(2)}) copy-start(s32[1,8]{1,0:T(1,128)} %param.16) | copy-start | bytes 100
  7.2 12.3 %copy-start.5 = (s32[64]{0:T(128)S(1)}, s32[64]{0:T(128)}, u32[]{:S(2)}) copy-start(s32[64]{0:T(128)} %param.17) | copy-start | bytes 772
  7.2 13.0 %copy-start.2 = (bf16[1,128,1024]{2,1,0:T(8,128)(2,1)S(1)}, bf16[1,128,1024]{2,1,0:T(8,128)(2,1)}, u32[]{:S(2)}) copy-start(bf16[1,128,1024]{2,1,0:T(8,128)(2,1)} %param.12) | copy-start | bytes 786436
  7.2 68.0 %all-gather.3.cloned.1.call-start = ((), (), s32[]{:S(2)}) async-start(), calls=%async_computation.6 | async-start | bytes 1081344 | tf_op jit(solution)/shard_map/all_gather | solution.py:31
  7.9 14.3 %copy-start.3 = (bf16[1,128,1024]{2,1,0:T(8,128)(2,1)S(1)}, bf16[1,128,1024]{2,1,0:T(8,128)(2,1)}, u32[]{:S(2)}) copy-start(bf16[1,128,1024]{2,1,0:T(8,128)(2,1)} %param.15) | copy-start | bytes 786436
  10.0 65.2 %all-to-all-start = ((bf16[32,128,128]{2,1,0:T(8,128)(2,1)}), bf16[32,128,128]{2,1,0:T(8,128)(2,1)}, u32[]{:S(2)}, u32[]{:S(2)}) async-start(bf16[32,128,128]{2,1,0:T(8,128)(2,1)} %stack.3), calls=%async_computation | async-start | bytes 2097152 | tf_op jit(solution)/shard_map/all_to_all | solution.py:28
  19.2 284.9 %reduce-scatter.6.cloned.1.call-start = ((), (), s32[]{:S(2)}) async-start(), calls=%async_computation.4 | async-start | bytes 4325376 | tf_op jit(solution)/shard_map/reduce_scatter | solution.py:91
  171.9 297.6 %reduce-scatter.8.cloned.1.call-start = ((), (), s32[]{:S(2)}) async-start(), calls=%async_computation.5 | async-start | bytes 8650752 | tf_op jit(solution)/shard_map/reduce_scatter | solution.py:99
  310.7 162.6 %copy-start.1 = (f32[128,256]{1,0:T(8,128)S(1)}, f32[128,256]{1,0:T(8,128)}, u32[]{:S(2)}) copy-start(f32[128,256]{1,0:T(8,128)} %reduce-scatter.6.cloned.1.call-done) | copy-start | bytes 393220
  310.7 261.2 %reduce-scatter.10.cloned.1.call-start = ((), (), s32[]{:S(2)}) async-start(), calls=%async_computation.7 | async-start | bytes 294912
Sparse Core Ops, SparseCore 0:
  9.9 65.2 all-gather.2
  172.1 131.9 reduce-scatter.5
  310.8 158.7 reduce-scatter.7
  473.2 98.5 reduce-scatter.9
